TPU v7x, 512 devices: a whole 4x4x16 slice. The times are simulated.
512 devices in a mesh: section: 8 (over x, core), expert: 8 (over z_lo), dp: 8 (over y, z_hi).
Axes of the slice: x: 4, y: 4, z: 16 (z_hi: 2, z_lo: 8; z = z_hi * 8 + z_lo), core: 2. Of those that a mesh axis runs over, the one named last changes fastest.
Arguments:
- layer_input: bfloat16 [8, 8192, 2048], P('section', ('expert', 'dp')), may hold values from -6 to 6
- output_grad: bfloat16 [8, 8192, 2048], P('section', ('expert', 'dp')), may hold values from -6 to 6
- expert_ids: int32 [8, 8192], P('section', ('expert', 'dp')), may hold values from 0 to 63, as said below
- w_gate: bfloat16 [8, 2048, 8192], P('section', None, ('expert', 'dp')), may hold values from -0.125 to 0.125
- w_up: bfloat16 [8, 2048, 8192], P('section', None, ('expert', 'dp')), may hold values from -0.125 to 0.125
- w_down: bfloat16 [8, 2048, 8192], P('section', None, ('expert', 'dp')), may hold values from -0.0625 to 0.0625
Outputs:
- input_grad: bfloat16 [8, 8192, 2048], P('section', ('expert', 'dp'))
- grad_gate: bfloat16 [8, 2048, 8192], P('section', None, ('expert', 'dp'))
- grad_up: bfloat16 [8, 2048, 8192], P('section', None, ('expert', 'dp'))
- grad_down: bfloat16 [8, 2048, 8192], P('section', None, ('expert', 'dp'))
Inputs may be any that keep to these rules, and one draw needn't show every extreme that they name: `expert_ids`: expert 0 is the expert of these weights. Every device's 128 tokens name expert 0 between 1 and 8 times, and on every section some device names it exactly 8 times.
All inputs are finite; a program needn't handle non-finite values.
Results may differ from a plain program's by a relative error of at most 0.0065.
Values may be sent and summed in bfloat16 or wider, within the bound.
A program may use at most 64 MiB of HBM per device.

v0:
```python
import jax
import jax.numpy as jnp
from jax import lax
from jax.sharding import PartitionSpec as P

SLOT = 8
GROUP = ("expert", "dp")


def shifted(value, axis, steps):
    count = lax.axis_size(axis)
    pairs = [(source, (source + steps) % count) for source in range(count)]
    return lax.ppermute(value, axis, pairs)


def body(layer_input, output_grad, expert_ids, w_gate, w_up, w_down):
    inputs = layer_input[0]
    grads = output_grad[0]
    routes = expert_ids[0]
    chosen = (routes == 0).astype(jnp.int32)
    order = jnp.arange(chosen.shape[0], dtype=jnp.int32)
    within = jnp.sum(jnp.where(order[None, :] < order[:, None], chosen[None, :], 0), axis=1)
    target = jnp.where(chosen > 0, within, SLOT)
    places = jnp.arange(SLOT, dtype=jnp.int32)
    match = (target[None, :] == places[:, None]).astype(jnp.bfloat16)
    send_x = jnp.dot(match, inputs, preferred_element_type=jnp.float32).astype(jnp.bfloat16)
    send_dy = jnp.dot(match, grads, preferred_element_type=jnp.float32).astype(jnp.bfloat16)
    moved_grads = shifted(grads, "section", -1)
    moved_match = shifted(match, "section", -1)
    rows = lax.all_gather(jnp.stack([send_x, send_dy]), GROUP, axis=1, tiled=True)
    x_rows, dy_rows = (rows[0], rows[1])
    w_both = jnp.concatenate([w_gate[0], w_up[0]], axis=1)
    both = jnp.dot(x_rows, w_both, preferred_element_type=jnp.float32)
    width = w_gate.shape[2]
    gate, upper = (both[:, :width], both[:, width:])
    sigma = jax.nn.sigmoid(gate)
    active = gate * sigma
    hidden = (active * upper).astype(jnp.bfloat16)
    d_hidden = jnp.dot(dy_rows, w_down[0], preferred_element_type=jnp.float32)
    d_gate = (d_hidden * upper * sigma * (1.0 + gate * (1.0 - sigma))).astype(jnp.bfloat16)
    d_up = (d_hidden * active).astype(jnp.bfloat16)
    d_both = jnp.concatenate([d_gate, d_up], axis=1)
    back_dims = (((1,), (1,)), ((), ()))
    d_part = lax.dot_general(d_both, w_both, back_dims, preferred_element_type=jnp.float32)
    d_rows = lax.psum_scatter(d_part.astype(jnp.bfloat16), GROUP, scatter_dimension=0, tiled=True)
    d_rows = shifted(d_rows, "section", -1)
    row_dims = (((0,), (0,)), ((), ()))
    part_both = lax.dot_general(
        x_rows, d_both, row_dims, preferred_element_type=jnp.float32
    ).astype(jnp.bfloat16)
    part_down = lax.dot_general(
        dy_rows, hidden, row_dims, preferred_element_type=jnp.float32
    ).astype(jnp.bfloat16)
    term = lax.dot_general(
        moved_match, d_rows, (((0,), (0,)), ((), ())), preferred_element_type=jnp.float32
    )
    token_grad = (moved_grads.astype(jnp.float32) + term).astype(jnp.bfloat16)
    return (
        token_grad[None],
        part_both[None, :, :width],
        part_both[None, :, width:],
        part_down[None],
    )


def solution(mesh):
    rows = P("section", ("expert", "dp"), None)
    weights = P("section", None, ("expert", "dp"))
    in_specs = (rows, rows, P("section", ("expert", "dp")), weights, weights, weights)
    out_specs = (rows, weights, weights, weights)
    return jax.shard_map(body, mesh=mesh, in_specs=in_specs, out_specs=out_specs, check_vma=False)
```

profile of v0, /device:TPU:65, one launch (start us, length us, event | category | flops | bytes accessed | tf_op | source)
XLA Modules:
  0.0 1204.5 jit_solution(17072513962563415594)
XLA Ops:
  7.2 0.0 all-gather.2.cloned.1.call-start
  7.2 0.7 fusion.14
  7.9 0.1 select_reduce_fusion
  8.0 0.7 fusion.13
  8.7 1.2 fusion.2
  9.9 1.2 fusion.1
  11.2 0.6 pad_maximum_fusion.6
  11.8 0.0 all-gather.2.cloned.1.call-update
  11.8 0.0 reduce-scatter.2.cloned.1.call-start
  11.9 588.9 %all-gather.2.cloned.1.call-done = bf16[2,512,2048]{2,1,0:T(8,128)(2,1)} async-done(((bf16[2,8,2048]{2,1,0:T(8,128)(2,1)}), bf16[2,512,2048]{2,1,0:T(8,128)(2,1)}) %all-gather.2.cloned.1.call-update) | async-done | bytes 4194320 | tf_op jit(solution)/shard_map/all_gather | solution.py:30
  600.8 2.7 fusion.4
  603.5 0.4 copy-done.4
  603.9 0.9 multiply_convert_fusion.2
  604.8 0.2 copy-done.1
  605.0 0.2 copy-done.2
  605.1 2.1 convolution_convert_fusion
  607.3 48.0 %collective-permute-start.1 = (bf16[8,128]{1,0:T(8,128)(2,1)S(1)}, bf16[8,128]{1,0:T(8,128)(2,1)S(1)}, u32[]{:S(2)}, u32[]{:S(2)}) collective-permute-start(bf16[8,128]{1,0:T(8,128)(2,1)S(1)} %fusion.10), channel_id=1, source_target_pairs={{0,448},{64,0},{128,64},{192,128},{256,192},{320,256},{384,320},{4... | collective-permute-start | bytes 6152 | tf_op jit(solution)/shard_map/ppermute | solution.py:13
  655.2 1.0 collective-permute-start
  656.2 2.4 convolution_convert_fusion.1
  658.6 1.0 slice_bitcast_fusion.6
  659.6 466.6 %reduce-scatter.2.cloned.1.call-done = bf16[8,2048]{1,0:T(8,128)(2,1)} async-done(((bf16[512,2048]{1,0:T(8,128)(2,1)}), bf16[8,2048]{1,0:T(8,128)(2,1)}) %reduce-scatter.2.cloned.1.call-update) | async-done | bytes 32784 | tf_op jit(solution)/shard_map/reduce_scatter | solution.py:45
  1126.2 67.2 %collective-permute-start.2 = (bf16[8,2048]{1,0:T(8,128)(2,1)}, bf16[8,2048]{1,0:T(8,128)(2,1)S(1)}, u32[]{:S(2)}, u32[]{:S(2)}) collective-permute-start(bf16[8,2048]{1,0:T(8,128)(2,1)} %reduce-scatter.2.cloned.1.call-done), channel_id=1, source_target_pairs={{0,448},{64,0},{128,64},{192,128},{256,192},{320,256},{384,320},{4... | collective-permute-start | bytes 98312 | tf_op jit(solution)/shard_map/ppermute | solution.py:13
  1193.4 3.2 fusion
  1196.6 1.1 fusion.5
  (12 shorter events, 0.0 us)
Async XLA Ops:
  7.2 596.4 %copy-start = (bf16[1,2048,128]{2,1,0:T(8,128)(2,1)S(1)}, bf16[1,2048,128]{2,1,0:T(8,128)(2,1)}, u32[]{:S(2)}) copy-start(bf16[1,2048,128]{2,1,0:T(8,128)(2,1)} %param.11) | copy-start | bytes 1572868
  7.2 593.6 %all-gather.2.cloned.1.call-start = ((), (), s32[]{:S(2)}) async-start(), calls=%async_computation.1 | async-start | bytes 4259840 | tf_op jit(solution)/shard_map/all_gather | solution.py:30
  11.8 1114.4 %reduce-scatter.2.cloned.1.call-start = ((), (), s32[]{:S(2)}) async-start(), calls=%async_computation.2 | async-start | bytes 2129920 | tf_op jit(solution)/shard_map/reduce_scatter | solution.py:45
  600.8 3.1 copy-start.4
  603.9 1.0 copy-start.1
  603.9 1.2 copy-start.2
  607.2 48.0 %copy-start.3 = (bf16[1,128,2048]{2,1,0:T(8,128)(2,1)S(1)}, bf16[1,128,2048]{2,1,0:T(8,128)(2,1)}, u32[]{:S(2)}) copy-start(bf16[1,128,2048]{2,1,0:T(8,128)(2,1)} %param.7) | copy-start | bytes 1572868
  607.3 589.3 %collective-permute-start.1 = (bf16[8,128]{1,0:T(8,128)(2,1)S(1)}, bf16[8,128]{1,0:T(8,128)(2,1)S(1)}, u32[]{:S(2)}, u32[]{:S(2)}) collective-permute-start(bf16[8,128]{1,0:T(8,128)(2,1)S(1)} %fusion.10), channel_id=1, source_target_pairs={{0,448},{64,0},{128,64},{192,128},{256,192},{320,256},{384,320},{4... | collective-permute-start | bytes 6152 | tf_op jit(solution)/shard_map/ppermute | solution.py:13
  655.2 541.3 %collective-permute-start = (bf16[128,2048]{1,0:T(8,128)(2,1)S(1)}, bf16[128,2048]{1,0:T(8,128)(2,1)S(1)}, u32[]{:S(2)}, u32[]{:S(2)}) collective-permute-start(bf16[128,2048]{1,0:T(8,128)(2,1)S(1)} %bitcast.47), channel_id=1, source_target_pairs={{0,448},{64,0},{128,64},{192,128},{256,192},{320,256},{384,320},{4... | collective-permute-start | bytes 1572872 | tf_op jit(solution)/shard_map/ppermute | solution.py:13
  1126.2 70.4 %collective-permute-start.2 = (bf16[8,2048]{1,0:T(8,128)(2,1)}, bf16[8,2048]{1,0:T(8,128)(2,1)S(1)}, u32[]{:S(2)}, u32[]{:S(2)}) collective-permute-start(bf16[8,2048]{1,0:T(8,128)(2,1)} %reduce-scatter.2.cloned.1.call-done), channel_id=1, source_target_pairs={{0,448},{64,0},{128,64},{192,128},{256,192},{320,256},{384,320},{4... | collective-permute-start | bytes 98312 | tf_op jit(solution)/shard_map/ppermute | solution.py:13
Sparse Core Ops, SparseCore 0:
  11.9 588.7 all-gather.1
  607.4 518.7 reduce-scatter.1
where the time goes:
time: 1200 us
  waiting for transfers between devices  1060 us (88%)
  starting transfers between devices  116 us (10%)
  matrix products  14.8 us (1%)
  between operations  14.1 us (1%)
    all_gather x1, waiting for transfers between devices, body(): lax.all_gather(jnp.stack([send_x, send_dy]), GROUP, axis=1, tiled=True)  589 us
    reduce_scatter x1, waiting for transfers between devices, body(): lax.psum_scatter(d_part.astype(jnp.bfloat16), GROUP, scatter_dimension=0,...  467 us
    ppermute x3, starting transfers between devices, shifted(): return lax.ppermute(value, axis, pairs)  116 us
  transfers between devices with their start and end apart: 5, of which 2 were waited for; matrix products, arithmetic and copies ran while one was open for 1% of the time, Pallas kernels for 0%

commit v1 on v0

--- a/solution.py
+++ b/solution.py
@@ -27,7 +27,10 @@
     send_dy = jnp.dot(match, grads, preferred_element_type=jnp.float32).astype(jnp.bfloat16)
     moved_grads = shifted(grads, "section", -1)
     moved_match = shifted(match, "section", -1)
-    rows = lax.all_gather(jnp.stack([send_x, send_dy]), GROUP, axis=1, tiled=True)
+    rows = jnp.concatenate(
+        lax.all_to_all(jnp.stack(lax.psum(1, GROUP) * [jnp.stack([send_x, send_dy])]), GROUP, 0, 0),
+        axis=1,
+    )
     x_rows, dy_rows = (rows[0], rows[1])
     w_both = jnp.concatenate([w_gate[0], w_up[0]], axis=1)
     both = jnp.dot(x_rows, w_both, preferred_element_type=jnp.float32)

time: 1200 us -> 780 us (0.65)
  waiting for transfers between devices: 1060 us -> 482 us
  blocking collectives: 0 us -> 198 us
  starting transfers between devices: 116 us -> 68.8 us
    all_gather x1 -> x0, waiting for transfers between devices: 589 us -> none  [body(): lax.all_gather(jnp.stack([send_x, send_dy]), GROUP, axis=1, tiled=True)]
    all_to_all x0 -> x1, blocking collectives: none -> 198 us  [body(): lax.all_to_all(jnp.stack(lax.psum(1, GROUP) * [jnp.stack([send_x, send_dy...]
    ppermute x3, starting transfers between devices: 116 us -> 68.8 us  [shifted(): return lax.ppermute(value, axis, pairs)]
    reduce_scatter x1, waiting for transfers between devices: 467 us -> 482 us  [body(): lax.psum_scatter(d_part.astype(jnp.bfloat16), GROUP, scatter_dimension=0,...]
  transfers between devices with their start and end apart: 5 -> 4, of which waited for: 2 -> 1; matrix products, arithmetic and copies ran while one was open for 1% -> 1% of each run, Pallas kernels for 0% -> 0%
where the time goes in v1:
time: 780 us
  waiting for transfers between devices  482 us (62%)
  blocking collectives  198 us (25%)
  starting transfers between devices  68.8 us (9%)
  between operations  14.1 us (2%)
  matrix products  12.8 us (2%)
    reduce_scatter x1, waiting for transfers between devices, body(): lax.psum_scatter(d_part.astype(jnp.bfloat16), GROUP, scatter_dimension=0,...  482 us
    all_to_all x1, blocking collectives, body(): lax.all_to_all(jnp.stack(lax.psum(1, GROUP) * [jnp.stack([send_x, send_dy...  198 us
    ppermute x3, starting transfers between devices, shifted(): return lax.ppermute(value, axis, pairs)  68.8 us
  transfers between devices with their start and end apart: 4, of which 1 were waited for; matrix products, arithmetic and copies ran while one was open for 1% of the time, Pallas kernels for 0%

profile of v1, /device:TPU:65, one launch (start us, length us, event | category | flops | bytes accessed | tf_op | source)
XLA Modules:
  0.0 780.0 jit_solution(6523241737964046626)
XLA Ops:
  7.2 0.0 copy-start
  7.2 0.0 reduce-scatter.2.cloned.1.call-start
  7.2 0.7 fusion.14
  7.9 0.1 select_reduce_fusion
  8.0 0.7 fusion.13
  8.7 1.2 fusion.1
  9.9 1.2 fusion.2
  11.2 0.5 stack.11
  11.7 0.0 copy-start.2
  11.7 0.0 copy-start.3
  11.7 197.7 %all_to_all.5 = bf16[64,2,8,2048]{3,2,1,0:T(8,128)(2,1)S(1)} all-to-all(bf16[64,2,8,2048]{3,2,1,0:T(8,128)(2,1)S(1)} %stack.11), channel_id=1, replica_groups=mesh['section'=8,'expert'=8,'dp'=8] {'expert','dp'}, dimensions={0} | all-to-all | bytes 8388608 | tf_op jit(solution)/shard_map/all_to_all | solution.py:31
  209.4 0.8 fusion.4
  210.2 1.2 copy-done.1
  211.4 0.9 multiply_convert_fusion.2
  212.2 2.1 convolution_convert_fusion
  214.3 0.0 reduce-scatter.2.cloned.1.call-update
  214.4 6.0 collective-permute-start.1
  220.3 1.0 collective-permute-start
  221.3 2.4 convolution_convert_fusion.1
  223.7 1.0 slice_bitcast_fusion.6
  224.7 482.2 %reduce-scatter.2.cloned.1.call-done = bf16[8,2048]{1,0:T(8,128)(2,1)} async-done(((bf16[512,2048]{1,0:T(8,128)(2,1)}), bf16[8,2048]{1,0:T(8,128)(2,1)}) %reduce-scatter.2.cloned.1.call-update) | async-done | bytes 32784 | tf_op jit(solution)/shard_map/reduce_scatter | solution.py:48
  707.0 61.8 %collective-permute-start.2 = (bf16[8,2048]{1,0:T(8,128)(2,1)}, bf16[8,2048]{1,0:T(8,128)(2,1)S(1)}, u32[]{:S(2)}, u32[]{:S(2)}) collective-permute-start(bf16[8,2048]{1,0:T(8,128)(2,1)} %reduce-scatter.2.cloned.1.call-done), channel_id=1, source_target_pairs={{0,448},{64,0},{128,64},{192,128},{256,192},{320,256},{384,320},{4... | collective-permute-start | bytes 98312 | tf_op jit(solution)/shard_map/ppermute | solution.py:13
  768.8 3.2 fusion
  772.0 1.1 fusion.5
  (11 shorter events, 0.0 us)
Async XLA Ops:
  7.2 204.2 %copy-start = (bf16[1,2048,128]{2,1,0:T(8,128)(2,1)S(1)}, bf16[1,2048,128]{2,1,0:T(8,128)(2,1)}, u32[]{:S(2)}) copy-start(bf16[1,2048,128]{2,1,0:T(8,128)(2,1)} %param.11) | copy-start | bytes 1572868
  7.2 699.8 %reduce-scatter.2.cloned.1.call-start = ((), (), s32[]{:S(2)}) async-start(), calls=%async_computation.2 | async-start | bytes 2129920 | tf_op jit(solution)/shard_map/reduce_scatter | solution.py:48
  11.7 197.7 %copy-start.2 = (bf16[1,2048,128]{2,1,0:T(8,128)(2,1)S(1)}, bf16[1,2048,128]{2,1,0:T(8,128)(2,1)}, u32[]{:S(2)}) copy-start(bf16[1,2048,128]{2,1,0:T(8,128)(2,1)} %param.10) | copy-start | bytes 1572868
  11.7 197.7 %copy-start.3 = (bf16[1,2048,128]{2,1,0:T(8,128)(2,1)S(1)}, bf16[1,2048,128]{2,1,0:T(8,128)(2,1)}, u32[]{:S(2)}) copy-start(bf16[1,2048,128]{2,1,0:T(8,128)(2,1)} %param.9) | copy-start | bytes 1572868
  209.4 1.9 copy-start.1
  214.3 6.0 copy-start.4
  214.4 557.6 %collective-permute-start.1 = (bf16[8,128]{1,0:T(8,128)(2,1)S(1)}, bf16[8,128]{1,0:T(8,128)(2,1)S(1)}, u32[]{:S(2)}, u32[]{:S(2)}) collective-permute-start(bf16[8,128]{1,0:T(8,128)(2,1)S(1)} %fusion.10), channel_id=1, source_target_pairs={{0,448},{64,0},{128,64},{192,128},{256,192},{320,256},{384,320},{4... | collective-permute-start | bytes 6152 | tf_op jit(solution)/shard_map/ppermute | solution.py:13
  220.3 551.6 %collective-permute-start = (bf16[128,2048]{1,0:T(8,128)(2,1)S(1)}, bf16[128,2048]{1,0:T(8,128)(2,1)S(1)}, u32[]{:S(2)}, u32[]{:S(2)}) collective-permute-start(bf16[128,2048]{1,0:T(8,128)(2,1)S(1)} %bitcast.52), channel_id=1, source_target_pairs={{0,448},{64,0},{128,64},{192,128},{256,192},{320,256},{384,320},{4... | collective-permute-start | bytes 1572872 | tf_op jit(solution)/shard_map/ppermute | solution.py:13
  707.0 65.0 %collective-permute-start.2 = (bf16[8,2048]{1,0:T(8,128)(2,1)}, bf16[8,2048]{1,0:T(8,128)(2,1)S(1)}, u32[]{:S(2)}, u32[]{:S(2)}) collective-permute-start(bf16[8,2048]{1,0:T(8,128)(2,1)} %reduce-scatter.2.cloned.1.call-done), channel_id=1, source_target_pairs={{0,448},{64,0},{128,64},{192,128},{256,192},{320,256},{384,320},{4... | collective-permute-start | bytes 98312 | tf_op jit(solution)/shard_map/ppermute | solution.py:13
Sparse Core Ops, SparseCore 0:
  214.5 492.4 reduce-scatter.1
